TPU v7x, 512 devices: a whole 4x8x8 slice. The times are simulated.
512 devices in a mesh: child: 2 (over x_hi), row: 16 (over z, x_lo), col: 16 (over y, core).
Axes of the slice: x: 4 (x_hi: 2, x_lo: 2; x = x_hi * 2 + x_lo), y: 8, z: 8, core: 2. Of those that a mesh axis runs over, the one named last changes fastest.
Arguments:
- contrib: float32 [2, 8192, 8192], P('child', 'row', 'col'), may hold values from -0.0625 to 0.0625
- assembled: float32 [2, 8192, 16384], P('child', 'row', 'col'), may hold values from -0.0625 to 0.0625
- pattern: int32 [64, 64], P('row', 'col'), may hold values 0 or 1
- omega: float32 [16384, 256], P('col', 'row'), may hold values from -6 to 6
- row_maps: int32 [2, 8192], P('child'), may hold values from 0 to 16383, as said below
- leaf_bounds: int32 [16], P('row'), may hold values from 448 to 576
Outputs:
- bases: float32 [16384, 256], P('row', ('child', 'col'))
- coupling: float32 [16, 2, 256, 256], P('row', None, ('child', 'col'))
Inputs may be any that keep to these rules, and one draw needn't show every extreme that they name: `row_maps`: for each child, entries k * 512 to (k + 1) * 512 - 1 are distinct, rising, and lie in k * 1024 to (k + 1) * 1024 - 1.
All inputs are finite; a program needn't handle non-finite values. No bound on the sum of `pattern` on one device may be relied on, other than what follows from the above.
Results may differ from a plain program's by a relative error of at most 0.0003.
Values sent between devices are 32-bit elements; how exact they have to be, the bound alone decides.
No kernel may reach another device: no remote copies, remote signals or barrier semaphores. Data moves between devices by JAX's collectives and lax.ppermute only.
A program may use at most 64 MiB of HBM per device.

v0:
```python
import jax
import jax.numpy as jnp
from jax import lax
from jax.sharding import PartitionSpec as P

R = 256
BT = 256
highest = lax.Precision.HIGHEST


def partner(block, axis, distance):
    count = lax.axis_size(axis)
    route = []
    for low in range(count):
        high = low | 1 << distance
        if high != low and high < count:
            route += [(low, high), (high, low)]
    return lax.ppermute(block, axis, route)


def window_leaves(window, leaf_bound, counts):
    window_rows = window.shape[0]
    upper = window_rows // 2 + window_rows // 16
    lower = window_rows // 2 - window_rows // 16
    positions = jnp.arange(window_rows, dtype=jnp.int32)
    first_leaf = (positions < leaf_bound)[:, None]
    head_rows = window[:upper]
    tail_rows = window[lower:]
    head_masked = jnp.where(first_leaf[:upper], head_rows, 0.0)
    tail_masked = jnp.where(first_leaf[lower:], 0.0, tail_rows)
    head_gram = jnp.dot(head_masked.T, head_rows, precision=highest)
    tail_gram = jnp.dot(tail_masked.T, tail_rows, precision=highest)
    factors = jnp.linalg.cholesky(jnp.stack([head_gram, tail_gram]) / counts)
    head_part = lax.linalg.triangular_solve(
        factors[0], head_rows, left_side=False, lower=True, transpose_a=True
    )
    tail_part = lax.linalg.triangular_solve(
        factors[1], tail_rows, left_side=False, lower=True, transpose_a=True
    )
    middle = jnp.where(first_leaf[lower:upper], head_part[lower:], tail_part[: upper - lower])
    whole = jnp.concatenate([head_part[:lower], middle, tail_part[upper - lower :]], axis=0)
    return (factors, whole)


def local(contrib, assembled, pattern, omega, row_maps, leaf_bounds):
    tile_rows = contrib.shape[1]
    tile_cols = contrib.shape[2]
    window_rows = omega.shape[0]
    slice_width = R // (2 * lax.axis_size("col"))
    row_pos = lax.axis_index("row")
    col_pos = lax.axis_index("col")
    half_pos = lax.axis_index("child")
    group_pos = half_pos * lax.axis_size("col") + col_pos
    zero_index = jnp.zeros((), jnp.int32)
    child_maps = row_maps[0]
    column_maps = (
        lax.dynamic_slice_in_dim(child_maps, col_pos * tile_cols, tile_cols) - col_pos * window_rows
    )
    target_maps = (
        lax.dynamic_slice_in_dim(child_maps, row_pos * tile_rows, tile_rows) - row_pos * window_rows
    )
    full_omega = lax.all_gather(omega, "row", axis=1, tiled=True)
    picked = jnp.take(full_omega, column_maps, axis=0)
    product = jnp.dot(contrib[0], picked, precision=highest)
    pattern_rows = lax.dynamic_slice_in_dim(
        pattern, half_pos * (tile_rows // BT), tile_rows // BT, 0
    ).astype(jnp.float32)
    masked = (
        assembled[0].reshape(tile_rows // BT, BT, window_rows // BT, BT)
        * pattern_rows[:, None, :, None]
    ).reshape(tile_rows, window_rows)
    sparse = jnp.dot(masked, full_omega, precision=highest)
    child_red, sparse_red = (
        lax.psum_scatter(
            product.reshape(tile_rows, 2, R // 2), "col", scatter_dimension=2, tiled=True
        ),
        lax.psum_scatter(
            sparse.reshape(tile_rows, 2, R // 2), "col", scatter_dimension=2, tiled=True
        ),
    )
    spread = jnp.zeros((window_rows, 2, slice_width), jnp.float32).at[target_maps].add(child_red)
    placed = lax.dynamic_update_slice(
        jnp.zeros((window_rows, 2, slice_width), jnp.float32),
        sparse_red,
        (half_pos * tile_rows, zero_index, zero_index),
    )
    samples = lax.psum_scatter(spread + placed, "child", scatter_dimension=1, tiled=True).reshape(
        window_rows, slice_width
    )
    leaf_bound = leaf_bounds[0]
    head_count = leaf_bound.astype(jnp.float32)
    tail_count = (window_rows - leaf_bound).astype(jnp.float32)
    counts = jnp.stack([head_count, tail_count])[:, None, None]
    window = lax.all_gather(samples, ("child", "col"), axis=1, tiled=True)
    factors, whole = window_leaves(window, leaf_bound, counts)
    bases = lax.dynamic_slice_in_dim(whole, group_pos * slice_width, slice_width, 1)
    own_cols = lax.dynamic_slice_in_dim(factors, group_pos * slice_width, slice_width, 2)
    sibling = partner(factors, "row", 0)
    coupling = jnp.einsum("lab,lac->lbc", own_cols, sibling, precision=highest)
    return (bases, coupling[None])


def solution(mesh):
    in_specs = (
        P("child", "row", "col"),
        P("child", "row", "col"),
        P("row", "col"),
        P("col", "row"),
        P("child", None),
        P("row"),
    )
    out_specs = (P("row", ("child", "col")), P("row", None, ("child", "col"), None))
    return jax.shard_map(local, mesh=mesh, in_specs=in_specs, out_specs=out_specs, check_vma=False)
```

profile of v0, /device:TPU:1, one launch (start us, length us, event | category | flops | bytes accessed | tf_op | source)
XLA Modules:
  0.0 525.0 jit_solution(18265540738242747835)
XLA Ops:
  7.2 0.7 all-gather.4.cloned.1.call-update
  8.0 0.7 fusion.39
  8.7 0.3 mul.45
  9.0 2.1 mul.46
  11.1 0.7 compare_select_fusion
  11.9 65.8 %all-gather.4.cloned.1.call-done = f32[1024,256]{0,1:T(8,128)} async-done(((f32[1024,16]{0,1:T(8,128)}), f32[1024,256]{0,1:T(8,128)}) %all-gather.4.cloned.1.call-update) | async-done | bytes 1048592 | tf_op jit(solution)/shard_map/all_gather | solution.py:62
  77.6 1.6 copy.55
  79.2 2.2 gather_fusion
  81.5 3.1 fusion.3
  84.6 1.2 copy.56
  85.9 4.7 fusion
  90.7 1.3 dynamic-slice.8
  92.6 118.2 %all-reduce.4.cloned.1.call-done = f32[512,2,128]{0,1,2:T(2,128)} async-done(((f32[512,2,128]{0,1,2:T(2,128)}), f32[512,2,128]{0,1,2:T(2,128)}) %all-reduce.4.cloned.1.call-update) | async-done | bytes 524304
  210.9 0.8 constant_dynamic-slice_fusion.6
  211.6 0.2 copy.57
  211.9 0.3 broadcast.161
  212.1 16.7 %scatter_fusion = f32[1024,2,8]{2,1,0:T(2,128)S(1)} fusion(f32[1024,2,8]{2,1,0:T(2,128)S(1)} %broadcast.161, s32[512]{0:T(512)S(1)} %bitcast.118, f32[512,2,8]{2,1,0:T(2,128)S(1)} %copy.57), kind=kCustom, calls=%fused_computation.1 | custom fusion | flops 8192 | bytes 100352 | tf_op jit(solution)/shard_map/scatter-add | solution.py:81
  228.9 0.2 copy.79
  229.0 42.9 %reduce-scatter.3.cloned.1.call-done = f32[512,2,8]{0,2,1:T(8,128)} async-done(((f32[512,2,128]{0,2,1:T(8,128)}), f32[512,2,8]{0,2,1:T(8,128)}) %reduce-scatter.3.cloned.1.call-update) | async-done | bytes 32784 | tf_op jit(solution)/shard_map/reduce_scatter | solution.py:77
  271.9 0.8 dynamic_update_slice.3
  272.7 0.2 copy.59
  273.0 1.0 copy.60
  274.1 0.2 all-gather.6.cloned.1.call-start
  274.3 19.7 %reduce-scatter.5.cloned.1.call-done = f32[1024,1,8]{0,2,1:T(8,128)} async-done(((f32[1024,2,8]{0,2,1:T(8,128)}), f32[1024,1,8]{0,2,1:T(8,128)}) %reduce-scatter.5.cloned.1.call-update) | async-done | bytes 32784 | tf_op jit(solution)/shard_map/reduce_scatter | solution.py:87
  294.0 1.4 copy.61
  296.4 84.6 %all-gather.6.cloned.1.call-done = f32[1024,1,256]{0,1,2:T(1,128)} async-done(((f32[1024,1,8]{0,1,2:T(1,128)}), f32[1024,1,256]{0,1,2:T(1,128)}) %all-gather.6.cloned.1.call-update) | async-done | bytes 1048592 | tf_op jit(solution)/shard_map/all_gather | solution.py:94
  381.1 3.1 fusion.48
  384.1 0.4 copy.80
  384.6 0.4 copy.81
  385.0 1.3 convolution_bitcast_fusion
  386.4 1.3 convolution_bitcast_fusion.1
  387.7 0.9 maximum_divide_fusion
  388.6 1.2 copy.66
  390.0 0.8 copy-done.3
  390.8 23.5 %custom-call.16 = f32[2,128,128]{2,1,0:T(8,128)S(1)} custom-call(f32[2,128,128]{2,1,0:T(8,128)S(1)} %cholesky.122), custom_call_target="Cholesky" | custom-call | tf_op jit(solution)/shard_map/jit(cholesky)/cholesky | solution.py:33
  414.3 19.7 %custom-call.17 = f32[2,1,128,128]{2,3,1,0:T(8,128)S(1)} custom-call(f32[2,1,128,128]{3,2,1,0:T(8,128)S(1)} %select_bitcast_fusion), custom_call_target="InvertDiagBlocksLowerTriangular" | custom-call | tf_op jit(solution)/shard_map/jit(cholesky)/cholesky | solution.py:33
  434.0 1.2 constant_dynamic-update-slice_fusion.1
  435.2 1.3 convolution_subtract_fusion.2
  436.5 23.7 %custom-call.18 = f32[2,128,128]{2,1,0:T(8,128)S(1)} custom-call(f32[2,128,128]{2,1,0:T(8,128)S(1)} %convolution_subtract_fusion.2), custom_call_target="Cholesky" | custom-call | tf_op jit(solution)/shard_map/jit(cholesky)/cholesky | solution.py:33
  460.2 0.2 compare_reduce_fusion
  460.4 0.1 select_select_fusion
  460.6 2.2 collective-permute-start
  462.9 4.0 while.4
  462.9 0.6 fusion.60
  463.5 1.4 bitcast_dynamic-update-slice_fusion.4
  464.9 0.6 fusion.60
  465.5 1.4 bitcast_dynamic-update-slice_fusion.4
  466.8 0.6 copy-done.4
  467.5 20.5 %custom-call.20 = f32[2,128,128]{1,2,0:T(8,128)S(1)} custom-call(f32[2,128,128]{2,1,0:T(8,128)} %copy-done.4), custom_call_target="InvertDiagBlocksLowerTriangular" | custom-call | tf_op jit(solution)/shard_map/triangular_solve/custom-call.0 | solution.py:34
  488.0 0.4 fusion.17
  488.4 1.2 convolution_subtract_fusion.1
  489.7 0.4 fusion.33
  490.1 4.0 while.5
  490.1 0.6 fusion.61
  490.7 1.4 bitcast_dynamic-update-slice_fusion.5
  492.1 0.6 fusion.61
  492.7 1.4 bitcast_dynamic-update-slice_fusion.5
  494.1 19.7 %custom-call.21 = f32[2,128,128]{1,2,0:T(8,128)S(1)} custom-call(f32[2,128,128]{2,1,0:T(8,128)S(1)} %get-tuple-element.18), custom_call_target="InvertDiagBlocksLowerTriangular" | custom-call | tf_op jit(solution)/shard_map/triangular_solve/custom-call.0 | solution.py:37
  513.8 0.4 fusion.15
  514.2 0.4 convolution_subtract_fusion
  514.6 0.4 fusion.31
  515.1 0.3 fusion.8
  515.4 0.8 copy.73
  516.2 2.3 convolution_bitcast_fusion.2
  (45 shorter events, 1.2 us)
Async XLA Ops:
  7.2 74.3 %copy-start = (f32[1,512,512]{2,1,0:T(8,128)S(1)}, f32[1,512,512]{2,1,0:T(8,128)}, u32[]{:S(2)}) copy-start(f32[1,512,512]{2,1,0:T(8,128)} %param.8) | copy-start | bytes 3145732
  7.2 70.5 %all-gather.4.cloned.1.call-start = ((), (), s32[]{:S(2)}) async-start(), calls=%async_computation.2 | async-start | bytes 1114112 | tf_op jit(solution)/shard_map/all_gather | solution.py:62
  7.9 202.9 %all-reduce.4.cloned.1.call-start = ((), (), s32[]{:S(2)}) async-start(), calls=%async_computation.6 | async-start | bytes 1048576
  81.5 4.4 copy-start.1
  85.8 186.1 %reduce-scatter.3.cloned.1.call-start = ((), (), s32[]{:S(2)}) async-start(), calls=%async_computation.3 | async-start | bytes 557056 | tf_op jit(solution)/shard_map/reduce_scatter | solution.py:77
  90.6 203.4 %reduce-scatter.5.cloned.1.call-start = ((), (), s32[]{:S(2)}) async-start(), calls=%async_computation.4 | async-start | bytes 98304 | tf_op jit(solution)/shard_map/reduce_scatter | solution.py:87
  274.1 107.0 %all-gather.6.cloned.1.call-start = ((), (), s32[]{:S(2)}) async-start(), calls=%async_computation.5 | async-start | bytes 1081344 | tf_op jit(solution)/shard_map/all_gather | solution.py:94
  390.0 0.8 copy-start.3
  460.6 55.6 %collective-permute-start = (f32[2,256,256]{2,1,0:T(8,128)S(1)}, f32[2,256,256]{2,1,0:T(8,128)}, u32[]{:S(2)}, u32[]{:S(2)}) collective-permute-start(f32[2,256,256]{2,1,0:T(8,128)S(1)} %select_select_fusion), channel_id=1, source_target_pairs={{0,16},{16,0},{32,48},{48,32},{64,80},{80,64},{96,112},{112,96},{1... | collective-permute-start | bytes 1572872 | tf_op jit(solution)/shard_map/ppermute | solution.py:18
  466.8 0.7 copy-start.4
  467.5 20.5 %copy-start.2 = (f32[256,256]{1,0:T(8,128)}, f32[256,256]{1,0:T(8,128)S(1)}, u32[]{:S(2)}) copy-start(f32[256,256]{1,0:T(8,128)S(1)} %get-tuple-element.164) | copy-start | bytes 786436
Sparse Core Ops, SparseCore 0:
  10.1 67.5 all-gather.3
  86.0 124.8 all-reduce.3
  213.9 57.9 reduce-scatter.2
  274.5 19.4 reduce-scatter.4
  297.8 83.2 all-gather.5
where the time goes:
time: 526 us; the launch traced here: 525 us
  waiting for transfers between devices  332 us (63%)
  other arithmetic  128 us (24%)
  local copies, waits for them, and re-layouts  28.5 us (5%)
  matrix products  18.5 us (4%)
  between operations  15.5 us (3%)
    unnamed x6, waiting for transfers between devices  119 us
    all_gather x1, waiting for transfers between devices, local(): window = lax.all_gather(samples, ('child', 'col'), axis=1, tiled=True)  84.6 us
    another operation x9, other arithmetic, window_leaves(): factors = jnp.linalg.cholesky(jnp.stack([head_gram, tail_gram]) / counts)  67.1 us
    all_gather x1, waiting for transfers between devices, local(): full_omega = lax.all_gather(omega, 'row', axis=1, tiled=True)  65.8 us
    reduce_scatter x1, waiting for transfers between devices, local(): lax.psum_scatter(sparse.reshape(tile_rows, 2, R // 2), 'col', scatter_dim...  42.9 us
    another operation x4, other arithmetic, window_leaves(): lax.linalg.triangular_solve(factors[0], head_rows, left_side=False, lower...  20.6 us
    reduce_scatter x1, waiting for transfers between devices, local(): lax.psum_scatter(spread + placed, 'child', scatter_dimension=1, tiled=True)  19.7 us
    another operation x2, other arithmetic, window_leaves(): lax.linalg.triangular_solve(factors[1], tail_rows, left_side=False, lower...  19.7 us
  transfers between devices with their start and end apart: 6, of which 5 were waited for; matrix products, arithmetic and copies ran while one was open for 15% of the time, Pallas kernels for 0%

commit v1 on v0

--- a/solution.py
+++ b/solution.py
@@ -59,7 +59,9 @@
     target_maps = (
         lax.dynamic_slice_in_dim(child_maps, row_pos * tile_rows, tile_rows) - row_pos * window_rows
     )
-    full_omega = lax.all_gather(omega, "row", axis=1, tiled=True)
+    full_omega = jnp.concatenate(
+        lax.all_to_all(jnp.stack([omega] * lax.axis_size("row")), "row", 0, 0), axis=1
+    )
     picked = jnp.take(full_omega, column_maps, axis=0)
     product = jnp.dot(contrib[0], picked, precision=highest)
     pattern_rows = lax.dynamic_slice_in_dim(

time: 526 us -> 484 us (0.920)
  waiting for transfers between devices: 332 us -> 275 us
  starting transfers between devices: 2.58 us -> 14.4 us
    all_gather x1 -> x0, waiting for transfers between devices: 65.8 us -> none  [local(): full_omega = lax.all_gather(omega, 'row', axis=1, tiled=True)]
    all_to_all x0 -> x1, waiting for transfers between devices: none -> 19.5 us  [local(): lax.all_to_all(jnp.stack([omega] * lax.axis_size('row')), 'row', 0, 0)]
    all_to_all x0 -> x1, starting transfers between devices: none -> 11.9 us  [local(): lax.all_to_all(jnp.stack([omega] * lax.axis_size('row')), 'row', 0, 0)]
    unnamed x6 -> x5, waiting for transfers between devices: 119 us -> 108 us
  transfers between devices with their start and end apart: 6 -> 6, of which waited for: 5 -> 5; matrix products, arithmetic and copies ran while one was open for 15% -> 17% of each run, Pallas kernels for 0% -> 0%
where the time goes in v1:
time: 484 us; the launch traced here: 483 us
  waiting for transfers between devices  275 us (57%)
  other arithmetic  127 us (26%)
  local copies, waits for them, and re-layouts  31.8 us (7%)
  matrix products  18.7 us (4%)
  between operations  15.5 us (3%)
  starting transfers between devices  14.4 us (3%)
    unnamed x5, waiting for transfers between devices  108 us
    all_gather x1, waiting for transfers between devices, local(): window = lax.all_gather(samples, ('child', 'col'), axis=1, tiled=True)  84.7 us
    another operation x9, other arithmetic, window_leaves(): factors = jnp.linalg.cholesky(jnp.stack([head_gram, tail_gram]) / counts)  67.1 us
    reduce_scatter x1, waiting for transfers between devices, local(): lax.psum_scatter(sparse.reshape(tile_rows, 2, R // 2), 'col', scatter_dim...  42.9 us
    another operation x4, other arithmetic, window_leaves(): lax.linalg.triangular_solve(factors[0], head_rows, left_side=False, lower...  20.6 us
    reduce_scatter x1, waiting for transfers between devices, local(): lax.psum_scatter(spread + placed, 'child', scatter_dimension=1, tiled=True)  19.9 us
    another operation x2, other arithmetic, window_leaves(): lax.linalg.triangular_solve(factors[1], tail_rows, left_side=False, lower...  19.7 us
    all_to_all x1, waiting for transfers between devices, local(): lax.all_to_all(jnp.stack([omega] * lax.axis_size('row')), 'row', 0, 0)  19.5 us
  transfers between devices with their start and end apart: 6, of which 5 were waited for; matrix products, arithmetic and copies ran while one was open for 17% of the time, Pallas kernels for 0%

profile of v1, /device:TPU:1, one launch (start us, length us, event | category | flops | bytes accessed | tf_op | source)
XLA Modules:
  0.0 482.9 jit_solution(6069594886435231908)
XLA Ops:
  7.2 2.0 stack.14
  9.2 11.9 %all-to-all-start = ((f32[16,1024,16]{1,2,0:T(8,128)}), f32[16,1024,16]{1,2,0:T(8,128)S(1)}, u32[]{:S(2)}, u32[]{:S(2)}) async-start(f32[16,1024,16]{1,2,0:T(8,128)} %stack.14), calls=%async_computation | async-start | bytes 2097152 | tf_op jit(solution)/shard_map/all_to_all | solution.py:63
  21.2 1.6 mul.45
  22.8 3.3 mul.46
  26.2 0.7 compare_select_fusion
  26.9 19.5 %all-to-all-done = f32[16,1024,16]{1,2,0:T(8,128)S(1)} async-done(((f32[16,1024,16]{1,2,0:T(8,128)}), f32[16,1024,16]{1,2,0:T(8,128)S(1)}, u32[]{:S(2)}, u32[]{:S(2)}) %all-to-all-start) | async-done | bytes 1048608 | tf_op jit(solution)/shard_map/all_to_all | solution.py:63
  46.4 0.3 copy.54
  46.7 2.2 gather_fusion
  49.0 3.0 fusion.3
  52.0 1.2 copy.55
  53.3 5.1 %fusion = f32[512,2,128]{0,2,1:T(8,128)} fusion(f32[2,128,1024]{2,1,0:T(8,128)S(1)} %bitcast.117, f32[1,512,1024]{2,1,0:T(8,128)} %param.9, f32[1,512,1024]{2,1,0:T(8,128)} %mul.46), kind=kOutput, calls=%fused_computation.6 | convolution fusion | flops 1611137024 | bytes 5767168 | tf_op jit(solution)/shard_map/dot_general | solution.py:74
  58.4 1.3 dynamic-slice.8
  60.4 108.3 %all-reduce.4.cloned.1.call-done = f32[512,2,128]{0,1,2:T(2,128)} async-done(((f32[512,2,128]{0,1,2:T(2,128)}), f32[512,2,128]{0,1,2:T(2,128)}) %all-reduce.4.cloned.1.call-update) | async-done | bytes 524304
  168.6 0.8 constant_dynamic-slice_fusion.6
  169.4 0.2 copy.56
  169.6 0.3 broadcast.163
  169.9 16.7 %scatter_fusion = f32[1024,2,8]{2,1,0:T(2,128)S(1)} fusion(f32[1024,2,8]{2,1,0:T(2,128)S(1)} %broadcast.163, s32[512]{0:T(512)S(1)} %bitcast.123, f32[512,2,8]{2,1,0:T(2,128)S(1)} %copy.56), kind=kCustom, calls=%fused_computation.1 | custom fusion | flops 8192 | bytes 100352 | tf_op jit(solution)/shard_map/scatter-add | solution.py:83
  186.6 0.2 copy.78
  186.8 42.9 %reduce-scatter.3.cloned.1.call-done = f32[512,2,8]{0,2,1:T(8,128)} async-done(((f32[512,2,128]{0,2,1:T(8,128)}), f32[512,2,8]{0,2,1:T(8,128)}) %reduce-scatter.3.cloned.1.call-update) | async-done | bytes 32784 | tf_op jit(solution)/shard_map/reduce_scatter | solution.py:79
  229.7 0.8 dynamic_update_slice.3
  230.4 0.2 copy.58
  230.8 1.0 copy.59
  231.8 0.2 all-gather.3.cloned.1.call-start
  232.1 19.9 %reduce-scatter.5.cloned.1.call-done = f32[1024,1,8]{0,2,1:T(8,128)} async-done(((f32[1024,2,8]{0,2,1:T(8,128)}), f32[1024,1,8]{0,2,1:T(8,128)}) %reduce-scatter.5.cloned.1.call-update) | async-done | bytes 32784 | tf_op jit(solution)/shard_map/reduce_scatter | solution.py:89
  251.9 1.4 copy.60
  254.3 84.7 %all-gather.3.cloned.1.call-done = f32[1024,1,256]{0,1,2:T(1,128)} async-done(((f32[1024,1,8]{0,1,2:T(1,128)}), f32[1024,1,256]{0,1,2:T(1,128)}) %all-gather.3.cloned.1.call-update) | async-done | bytes 1048592 | tf_op jit(solution)/shard_map/all_gather | solution.py:96
  339.0 3.1 fusion.48
  342.1 0.4 copy.79
  342.5 0.4 copy.80
  342.9 1.3 convolution_bitcast_fusion
  344.3 1.3 convolution_bitcast_fusion.1
  345.6 0.9 maximum_divide_fusion
  346.5 1.2 copy.65
  347.9 0.8 copy-done.2
  348.7 23.5 %custom-call.16 = f32[2,128,128]{2,1,0:T(8,128)S(1)} custom-call(f32[2,128,128]{2,1,0:T(8,128)S(1)} %cholesky.122), custom_call_target="Cholesky" | custom-call | tf_op jit(solution)/shard_map/jit(cholesky)/cholesky | solution.py:33
  372.2 19.7 %custom-call.17 = f32[2,1,128,128]{2,3,1,0:T(8,128)S(1)} custom-call(f32[2,1,128,128]{3,2,1,0:T(8,128)S(1)} %select_bitcast_fusion), custom_call_target="InvertDiagBlocksLowerTriangular" | custom-call | tf_op jit(solution)/shard_map/jit(cholesky)/cholesky | solution.py:33
  391.9 1.2 constant_dynamic-update-slice_fusion.1
  393.1 1.3 convolution_subtract_fusion.2
  394.4 23.7 %custom-call.18 = f32[2,128,128]{2,1,0:T(8,128)S(1)} custom-call(f32[2,128,128]{2,1,0:T(8,128)S(1)} %convolution_subtract_fusion.2), custom_call_target="Cholesky" | custom-call | tf_op jit(solution)/shard_map/jit(cholesky)/cholesky | solution.py:33
  418.1 0.2 compare_reduce_fusion
  418.3 0.1 select_select_fusion
  418.5 2.2 collective-permute-start
  420.8 4.0 while.4
  420.8 0.6 fusion.60
  421.4 1.4 bitcast_dynamic-update-slice_fusion.4
  422.8 0.6 fusion.60
  423.4 1.4 bitcast_dynamic-update-slice_fusion.4
  424.7 0.7 copy-done.3
  425.4 20.5 %custom-call.20 = f32[2,128,128]{1,2,0:T(8,128)S(1)} custom-call(f32[2,128,128]{2,1,0:T(8,128)} %copy-done.3), custom_call_target="InvertDiagBlocksLowerTriangular" | custom-call | tf_op jit(solution)/shard_map/triangular_solve/custom-call.0 | solution.py:34
  445.9 0.4 fusion.17
  446.3 1.2 convolution_subtract_fusion.1
  447.6 0.4 fusion.33
  448.0 4.0 while.5
  448.0 0.6 fusion.61
  448.6 1.4 bitcast_dynamic-update-slice_fusion.5
  450.0 0.6 fusion.61
  450.6 1.4 bitcast_dynamic-update-slice_fusion.5
  452.0 19.7 %custom-call.21 = f32[2,128,128]{1,2,0:T(8,128)S(1)} custom-call(f32[2,128,128]{2,1,0:T(8,128)S(1)} %get-tuple-element.18), custom_call_target="InvertDiagBlocksLowerTriangular" | custom-call | tf_op jit(solution)/shard_map/triangular_solve/custom-call.0 | solution.py:37
  471.7 0.4 fusion.15
  472.1 0.4 convolution_subtract_fusion
  472.5 0.4 fusion.31
  473.0 0.3 fusion.8
  473.3 0.8 copy.72
  474.1 2.3 convolution_bitcast_fusion.2
  (45 shorter events, 1.2 us)
Async XLA Ops:
  7.2 41.8 %copy-start = (f32[1,512,512]{2,1,0:T(8,128)S(1)}, f32[1,512,512]{2,1,0:T(8,128)}, u32[]{:S(2)}) copy-start(f32[1,512,512]{2,1,0:T(8,128)} %param.8) | copy-start | bytes 3145732
  7.2 14.0 %copy-start.4 = (s32[4,4]{1,0:T(4,128)S(1)}, s32[4,4]{1,0:T(4,128)}, u32[]{:S(2)}) copy-start(s32[4,4]{1,0:T(4,128)} %param.10) | copy-start | bytes 196
  9.2 37.2 %all-to-all-start = ((f32[16,1024,16]{1,2,0:T(8,128)}), f32[16,1024,16]{1,2,0:T(8,128)S(1)}, u32[]{:S(2)}, u32[]{:S(2)}) async-start(f32[16,1024,16]{1,2,0:T(8,128)} %stack.14), calls=%async_computation | async-start | bytes 2097152 | tf_op jit(solution)/shard_map/all_to_all | solution.py:63
  21.1 147.5 %all-reduce.4.cloned.1.call-start = ((), (), s32[]{:S(2)}) async-start(), calls=%async_computation.6 | async-start | bytes 1048576
  53.2 176.4 %reduce-scatter.3.cloned.1.call-start = ((), (), s32[]{:S(2)}) async-start(), calls=%async_computation.3 | async-start | bytes 557056 | tf_op jit(solution)/shard_map/reduce_scatter | solution.py:79
  58.4 193.6 %reduce-scatter.5.cloned.1.call-start = ((), (), s32[]{:S(2)}) async-start(), calls=%async_computation.4 | async-start | bytes 98304 | tf_op jit(solution)/shard_map/reduce_scatter | solution.py:89
  231.8 107.2 %all-gather.3.cloned.1.call-start = ((), (), s32[]{:S(2)}) async-start(), calls=%async_computation.5 | async-start | bytes 1081344 | tf_op jit(solution)/shard_map/all_gather | solution.py:96
  347.9 0.8 copy-start.2
  418.5 55.6 %collective-permute-start = (f32[2,256,256]{2,1,0:T(8,128)S(1)}, f32[2,256,256]{2,1,0:T(8,128)}, u32[]{:S(2)}, u32[]{:S(2)}) collective-permute-start(f32[2,256,256]{2,1,0:T(8,128)S(1)} %select_select_fusion), channel_id=1, source_target_pairs={{0,16},{16,0},{32,48},{48,32},{64,80},{80,64},{96,112},{112,96},{1... | collective-permute-start | bytes 1572872 | tf_op jit(solution)/shard_map/ppermute | solution.py:18
  424.7 0.7 copy-start.3
  425.4 20.5 %copy-start.1 = (f32[256,256]{1,0:T(8,128)}, f32[256,256]{1,0:T(8,128)S(1)}, u32[]{:S(2)}) copy-start(f32[256,256]{1,0:T(8,128)S(1)} %get-tuple-element.163) | copy-start | bytes 786436
Sparse Core Ops, SparseCore 0:
  53.4 115.2 all-reduce.3
  171.6 57.9 reduce-scatter.2
  232.4 19.4 reduce-scatter.4
  255.7 83.2 all-gather.2
